TPU v7x, 256 devices: a whole 4x4x8 slice. The times are simulated.
256 devices in a mesh: dp: 8 (over x, core), clus: 32 (over z, y).
Axes of the slice: x: 4, y: 4, z: 8, core: 2. Of those that a mesh axis runs over, the one named last changes fastest.
Arguments:
- activations: bfloat16 [1024, 12288], P('clus', 'dp'), may hold values from -6 to 6
- picks: int32 [1024, 48], replicated, may hold values from 0 to 383, all different within a row
- up_weight: bfloat16 [384, 12288, 128], P('clus', 'dp'), may hold values from -0.0546875 to 0.0546875
- up_bias: float32 [384, 128], P('clus'), may hold values from -3 to 3
- down_weight: bfloat16 [384, 128, 12288], P('clus', None, 'dp'), may hold values from -0.078125 to 0.078125
Outputs:
- layer_out: bfloat16 [1024, 12288], P('clus', 'dp')
Inputs may be any that keep to these rules, and one draw needn't show every extreme that they name: `picks`: each row names 48 distinct clusters; every cluster is named by some row.
All inputs are finite; a program needn't handle non-finite values.
Results may differ from a plain program's by a relative error of at most 0.012.
Values may be sent and summed in bfloat16 or wider, within the bound.
No kernel may reach another device: no remote copies, remote signals or barrier semaphores. Data moves between devices by JAX's collectives and lax.ppermute only.
A program may use at most 64 MiB of HBM per device.

v0:
```python
import jax
import jax.numpy as jnp
from jax import lax
from jax.sharding import PartitionSpec as P


def on_device(activations, picks, up_weight, up_bias, down_weight):
    tok_rows = activations.shape[0]
    clusters_here = up_weight.shape[0]
    ngroups = lax.axis_size("clus")
    own_index = lax.axis_index("clus")
    wanted = own_index * clusters_here + jnp.arange(clusters_here, dtype=jnp.int32)
    cluster_mask = jnp.any(picks[:, :, None] == wanted[None, None, :], axis=1).astype(jnp.float32)
    partial_pre = jnp.einsum(
        "rd,cdn->rcn",
        lax.all_gather(activations, "clus", axis=0, tiled=True),
        up_weight,
        preferred_element_type=jnp.float32,
    )
    summed = lax.psum(partial_pre, "dp")
    hidden = (jnp.maximum(summed + up_bias[None], 0.0) * cluster_mask[:, :, None]).astype(
        jnp.bfloat16
    )
    produced = jnp.einsum(
        "rcn,cnd->rd", hidden, down_weight, preferred_element_type=jnp.float32
    ).astype(jnp.bfloat16)
    returned = lax.all_to_all(produced, "clus", split_axis=0, concat_axis=0, tiled=True)
    combined = jnp.sum(returned.reshape(ngroups, tok_rows, -1).astype(jnp.float32), axis=0)
    return combined.astype(jnp.bfloat16)


def solution(mesh):
    placed = (P("clus", "dp"), P(), P("clus", "dp", None), P("clus", None), P("clus", None, "dp"))
    return jax.shard_map(
        on_device, mesh=mesh, in_specs=placed, out_specs=P("clus", "dp"), check_vma=False
    )
```

profile of v0, /device:TPU:8, one launch (start us, length us, event | category | flops | bytes accessed | tf_op | source)
XLA Modules:
  0.0 287.8 jit_solution(2460039226780015000)
XLA Ops:
  6.5 0.0 all-gather.2.cloned.1.call-start
  6.5 0.7 all-gather.2.cloned.1.call-update
  7.3 0.0 all-reduce.2.cloned.1.call-start
  7.3 84.3 %all-gather.2.cloned.1.call-done = bf16[1024,1536]{1,0:T(8,128)(2,1)} async-done(((bf16[32,1536]{1,0:T(8,128)(2,1)}), bf16[1024,1536]{1,0:T(8,128)(2,1)}) %all-gather.2.cloned.1.call-update) | async-done | bytes 3145744 | tf_op jit(solution)/shard_map/all_gather | solution.py:16
  91.6 9.7 %fusion = f32[1024,12,128]{2,0,1:T(8,128)} fusion(bf16[12,1536,128]{2,1,0:T(8,128)(2,1)} %param.7, bf16[1024,1536]{1,0:T(8,128)(2,1)} %all-gather.2.cloned.1.call-done), kind=kOutput, calls=%fused_computation.2 | convolution fusion | flops 4831838208 | bytes 14155776 | tf_op jit(solution)/shard_map/rd,cdn->rcn/dot_general | solution.py:14
  101.3 0.0 copy-start
  101.3 0.0 copy-start.1
  101.3 0.0 all-reduce.2.cloned.1.call-update
  101.3 0.9 copy-done
  102.2 0.4 compare_reduce_fusion
  102.7 86.0 %all-reduce.2.cloned.1.call-done = f32[1024,12,128]{2,0,1:T(8,128)} async-done(((f32[1024,12,128]{2,0,1:T(8,128)}), f32[1024,12,128]{2,0,1:T(8,128)}) %all-reduce.2.cloned.1.call-update) | async-done | bytes 6291472 | tf_op jit(solution)/shard_map/psum | solution.py:20
  188.7 0.0 copy-done.1
  188.7 8.6 %bitcast_convert_fusion = bf16[1024,1536]{1,0:T(8,128)(2,1)S(1)} fusion(bf16[12,128,1536]{2,1,0:T(8,128)(2,1)} %param.9, f32[1024,12,128]{2,0,1:T(8,128)} %all-reduce.2.cloned.1.call-done, f32[1024,12]{0,1:T(8,128)S(1)} %convert_element_type.15, f32[12,128]{1,0:T(8,128)S(1)} %copy-done.1), kind=kOutput, calls=%fused_computation | convolution fusion | flops 4839702528 | bytes 14211072 | tf_op jit(solution)/shard_map/rcn,cnd->rd/dot_general | solution.py:24
  197.3 82.6 %all_to_all.9 = bf16[32,32,1536]{2,1,0:T(8,128)(2,1)S(1)} all-to-all(bf16[32,32,1536]{2,1,0:T(8,128)(2,1)S(1)} %bitcast.8), channel_id=1, replica_groups=mesh['dp'=8,'clus'=32] {'clus'}, dimensions={0} | all-to-all | bytes 6291456 | tf_op jit(solution)/shard_map/all_to_all | solution.py:27
  279.9 1.1 reduce_sum.12
  (2 shorter events, 0.0 us)
Async XLA Ops:
  6.5 85.0 %all-gather.2.cloned.1.call-start = ((), (), s32[]{:S(2)}) async-start(), calls=%async_computation.1 | async-start | bytes 3244032 | tf_op jit(solution)/shard_map/all_gather | solution.py:16
  7.3 181.4 %all-reduce.2.cloned.1.call-start = ((), (), s32[]{:S(2)}) async-start(), calls=%async_computation.2 | async-start | bytes 12582912 | tf_op jit(solution)/shard_map/psum | solution.py:20
  101.3 0.9 copy-start
  101.3 87.4 %copy-start.1 = (f32[12,128]{1,0:T(8,128)S(1)}, f32[12,128]{1,0:T(8,128)}, u32[]{:S(2)}) copy-start(f32[12,128]{1,0:T(8,128)} %param.8) | copy-start | bytes 18436
Sparse Core Ops, SparseCore 0:
  9.9 81.5 all-gather.1
  101.4 87.1 all-reduce.1
where the time goes:
time: 288 us
  waiting for transfers between devices  171 us (59%)
  blocking collectives  82.6 us (29%)
  matrix products  18.4 us (6%)
  between operations  13.4 us (5%)
    psum x1, waiting for transfers between devices, on_device(): summed = lax.psum(partial_pre, 'dp')  86 us
    all_gather x1, waiting for transfers between devices, on_device(): lax.all_gather(activations, 'clus', axis=0, tiled=True)  84.3 us
    all_to_all x1, blocking collectives, on_device(): lax.all_to_all(produced, 'clus', split_axis=0, concat_axis=0, tiled=True)  82.6 us
    dot_general x1, matrix products, on_device(): jnp.einsum('rd,cdn->rcn', lax.all_gather(activations, 'clus', axis=0, til...  9.73 us
    dot_general x1, matrix products, on_device(): jnp.einsum('rcn,cnd->rd', hidden, down_weight, preferred_element_type=jnp...  8.65 us
  transfers between devices with their start and end apart: 2, of which 2 were waited for; matrix products, arithmetic and copies ran while one was open for 0% of the time, Pallas kernels for 0%

commit v1 on v0

v1 whole, which is shorter than its diff:
```python
import jax
import jax.numpy as jnp
from jax import lax
from jax.sharding import Mesh
from jax.sharding import PartitionSpec as P

F32, BF16 = jnp.float32, jnp.bfloat16


def spread(block, axis):
    peers = lax.axis_size(axis)
    return lax.all_to_all(
        jnp.broadcast_to(block[None], (peers,) + block.shape), axis, split_axis=0, concat_axis=0
    )


def exchange(blocks, axis):
    return lax.all_to_all(blocks, axis, split_axis=0, concat_axis=0)


def total(blocks):
    return jnp.sum(blocks.astype(F32), axis=0)


def swap(block):
    return lax.ppermute(block, "core", [(0, 1), (1, 0)])


def on_device(activations, picks, up_weight, up_bias, down_weight):
    nx, nz, ny = lax.axis_size("x"), lax.axis_size("z"), lax.axis_size("y")
    rows, width = activations.shape
    clusters, _, neurons = up_weight.shape
    tokens = nz * ny * rows
    cut = width // 2
    half = clusters // 2
    core, xi = lax.axis_index("core"), lax.axis_index("x")
    group = lax.axis_index("z") * ny + lax.axis_index("y")

    second = spread(activations[:, cut:], "y")
    first, second = lax.optimization_barrier((activations[:, :cut], second))
    x_b = lax.all_gather(second, "z", axis=0).reshape(tokens, -1)
    x_a = spread(spread(first, "z"), "y")
    x_a = jnp.transpose(x_a, (1, 0, 2, 3)).reshape(tokens, cut)

    def up(start):
        w = lax.dynamic_slice_in_dim(up_weight, start, half, 0)
        part = jnp.einsum("td,cdn->ctn", x_a, w[:, :cut], preferred_element_type=F32)
        return part + jnp.einsum("td,cdn->ctn", x_b, w[:, cut:], preferred_element_type=F32)

    mine, theirs = core * half, (1 - core) * half
    away = up(theirs).astype(BF16)
    here = up(mine)
    partial = (here + swap(away).astype(F32)).astype(BF16)
    partial = partial.reshape(half, nx, tokens // nx, neurons).transpose(1, 0, 2, 3)
    summed = total(exchange(partial, "x"))

    span = tokens // nx
    picked = lax.dynamic_slice_in_dim(picks, xi * span, span, 0)
    wanted = group * clusters + mine + jnp.arange(half, dtype=jnp.int32)
    mask = jnp.any(picked[None, :, :] == wanted[:, None, None], axis=-1).astype(F32)
    bias = lax.dynamic_slice_in_dim(up_bias, mine, half, 0)
    hidden = (jnp.maximum(summed + bias[:, None, :], 0.0) * mask[:, :, None]).astype(BF16)
    hidden = spread(hidden, "x")
    hidden = hidden.transpose(1, 0, 2, 3).reshape(half, tokens, neurons)
    other = swap(hidden)

    def down(low, high):
        w1 = lax.dynamic_slice_in_dim(down_weight[:, :, low:high], mine, half, 0)
        w2 = lax.dynamic_slice_in_dim(down_weight[:, :, low:high], theirs, half, 0)
        out = jnp.einsum("ctn,cnd->td", hidden, w1, preferred_element_type=F32)
        out = out + jnp.einsum("ctn,cnd->td", other, w2, preferred_element_type=F32)
        return out.astype(BF16)

    out_b = down(cut, width)
    scattered = lax.psum_scatter(out_b, "z", scatter_dimension=0, tiled=True)
    out_a = down(0, cut).reshape(nz, ny, rows, cut).transpose(1, 0, 2, 3)
    out_a = total(exchange(out_a, "y")).astype(BF16)
    out_a = total(exchange(out_a, "z")).astype(BF16)
    out_b = total(exchange(scattered.reshape(ny, rows, -1), "y")).astype(BF16)
    return jnp.concatenate([out_a, out_b], axis=1)


def solution(mesh):
    grid = Mesh(mesh.devices.reshape(4, 2, 8, 4), ("x", "core", "z", "y"))
    dp, clus = ("x", "core"), ("z", "y")
    placed = (P(clus, dp), P(), P(clus, dp, None), P(clus, None), P(clus, None, dp))
    return jax.shard_map(
        on_device, mesh=grid, in_specs=placed, out_specs=P(clus, dp), check_vma=False
    )
```

time: 288 us -> 200 us (0.69)
  waiting for transfers between devices: 171 us -> 39.9 us
  starting transfers between devices: 0.04 us -> 15.7 us
  blocking collectives: 82.6 us -> 97.4 us
  local copies, waits for them, and re-layouts: 0.89 us -> 7.47 us
  matrix products: 18.4 us -> 23.9 us
    psum x1 -> x0, waiting for transfers between devices: 86 us -> none  [on_device(): summed = lax.psum(partial_pre, 'dp')]
    all_gather x1, waiting for transfers between devices: 84.3 us -> 0.01 us  [on_device(): x_b = lax.all_gather(second, 'z', axis=0).reshape(tokens, -1)]
    all_to_all x0 -> x3, waiting for transfers between devices: none -> 38.8 us  [the longest x2 25.6 us: exchange(): return lax.all_to_all(blocks, axis, split_axis=0, concat_axis=0)]
    all_to_all x0 -> x3, starting transfers between devices: none -> 15.4 us  [the longest x2 9.38 us: exchange(): return lax.all_to_all(blocks, axis, split_axis=0, concat_axis=0)]
    all_to_all x1 -> x5, blocking collectives: 82.6 us -> 97.4 us  [the longest x3 56 us: spread(): lax.all_to_all(jnp.broadcast_to(block[None], (peers,) + block.shape), axi...]
    dot_general x2 -> x8, matrix products: 18.4 us -> 23.9 us  [the longest x2 8.04 us: up(): jnp.einsum('td,cdn->ctn', x_b, w[:, cut:], preferred_element_type=F32)]
  transfers between devices with their start and end apart: 2 -> 7, of which waited for: 2 -> 5; matrix products, arithmetic and copies ran while one was open for 0% -> 8% of each run, Pallas kernels for 0% -> 0%
where the time goes in v1:
time: 200 us
  blocking collectives  97.4 us (49%)
  waiting for transfers between devices  39.9 us (20%)
  matrix products  23.9 us (12%)
  starting transfers between devices  15.7 us (8%)
  between operations  13.6 us (7%)
  local copies, waits for them, and re-layouts  7.47 us (4%)
    all_to_all x3, blocking collectives, spread(): lax.all_to_all(jnp.broadcast_to(block[None], (peers,) + block.shape), axi...  56 us
    all_to_all x2, blocking collectives, exchange(): return lax.all_to_all(blocks, axis, split_axis=0, concat_axis=0)  41.4 us
    all_to_all x2, waiting for transfers between devices, exchange(): return lax.all_to_all(blocks, axis, split_axis=0, concat_axis=0)  25.6 us
    all_to_all x1, waiting for transfers between devices, spread(): lax.all_to_all(jnp.broadcast_to(block[None], (peers,) + block.shape), axi...  13.2 us
    all_to_all x2, starting transfers between devices, exchange(): return lax.all_to_all(blocks, axis, split_axis=0, concat_axis=0)  9.38 us
    dot_general x2, matrix products, up(): jnp.einsum('td,cdn->ctn', x_b, w[:, cut:], preferred_element_type=F32)  8.04 us
    dot_general x2, matrix products, up(): jnp.einsum('td,cdn->ctn', x_a, w[:, :cut], preferred_element_type=F32)  7.18 us
    all_to_all x1, starting transfers between devices, spread(): lax.all_to_all(jnp.broadcast_to(block[None], (peers,) + block.shape), axi...  6.02 us
  transfers between devices with their start and end apart: 7, of which 5 were waited for; matrix products, arithmetic and copies ran while one was open for 8% of the time, Pallas kernels for 0%

profile of v1, /device:TPU:8, one launch (start us, length us, event | category | flops | bytes accessed | tf_op | source)
XLA Modules:
  0.0 199.6 jit_solution(10683740273617992272)
XLA Ops:
  6.5 0.0 copy-start
  6.5 0.0 all-gather.3.cloned.1.call-start
  6.5 0.9 fusion.25
  7.4 10.1 %all_to_all.40 = bf16[4,32,768]{2,1,0:T(8,128)(2,1)} all-to-all(bf16[4,32,768]{2,1,0:T(8,128)(2,1)S(1)} %broadcast_in_dim.8), channel_id=1, replica_groups=mesh['x'=4,'core'=2,'z'=8,'y'=4] {'y'}, dimensions={0} | all-to-all | bytes 393216 | tf_op jit(solution)/shard_map/all_to_all | solution.py:12
  17.5 0.0 all-gather.3.cloned.1.call-update
  17.6 23.0 %all_to_all.41 = bf16[8,32,768]{2,1,0:T(8,128)(2,1)S(1)} all-to-all(bf16[8,32,768]{2,1,0:T(8,128)(2,1)S(1)} %broadcast_in_dim.9), channel_id=1, replica_groups=mesh['x'=4,'core'=2,'z'=8,'y'=4] {'z'}, dimensions={0} | all-to-all | bytes 786432 | tf_op jit(solution)/shard_map/all_to_all | solution.py:12
  40.6 1.3 broadcast_in_dim.10
  41.9 6.0 %all-to-all-start.2 = ((bf16[4,8,32,768]{3,2,1,0:T(8,128)(2,1)}), bf16[4,8,32,768]{3,2,1,0:T(8,128)(2,1)S(1)}, u32[]{:S(2)}, u32[]{:S(2)}) async-start(bf16[4,8,32,768]{3,2,1,0:T(8,128)(2,1)} %broadcast_in_dim.10), calls=%async_computation.2 | async-start | bytes 3145728 | tf_op jit(solution)/shard_map/all_to_all | solution.py:12
  48.0 13.2 %all-to-all-done.2 = bf16[4,8,32,768]{3,2,1,0:T(8,128)(2,1)S(1)} async-done(((bf16[4,8,32,768]{3,2,1,0:T(8,128)(2,1)}), bf16[4,8,32,768]{3,2,1,0:T(8,128)(2,1)S(1)}, u32[]{:S(2)}, u32[]{:S(2)}) %all-to-all-start.2) | async-done | bytes 1572896 | tf_op jit(solution)/shard_map/all_to_all | solution.py:12
  61.2 0.1 copy.19
  61.3 4.4 %fusion.5 = f32[6,128,1024]{2,1,0:T(8,128)} fusion(bf16[1024,768,1]{1,0,2:T(8,128)(2,1)S(1)} %bitcast.55, bf16[12,1536,128]{2,1,0:T(8,128)(2,1)} %param.7, s32[]{:T(128)S(6)} %select_n.7), kind=kOutput, calls=%fused_computation.12 | convolution fusion | flops 1207959552 | bytes 5898244 | tf_op jit(solution)/shard_map/td,cdn->ctn/dot_general | solution.py:47
  65.6 0.0 all-gather.3.cloned.1.call-done
  65.7 5.3 %fusion.3 = bf16[6,1024,128]{1,2,0:T(8,128)(2,1)} fusion(f32[6,128,1024]{2,1,0:T(8,128)} %fusion.5, bf16[1024,768,1]{1,0,2:T(8,128)(2,1)} %bitcast.60, bf16[12,1536,128]{2,1,0:T(8,128)(2,1)} %param.7, s32[]{:T(128)S(6)} %select_n.7, s32[]{:T(128)S(6)} %add.78), kind=kOutput, calls=%fused_computation.10 | convolution fusion | flops 1209532416 | bytes 7471112 | tf_op jit(solution)/shard_map/td,cdn->ctn/dot_general | solution.py:48
  71.0 0.0 collective-permute-start
  71.0 0.0 copy-start.4
  71.0 2.8 %fusion.8 = f32[6,128,1024]{2,1,0:T(8,128)S(1)} fusion(bf16[1024,768,1]{1,0,2:T(8,128)(2,1)S(1)} %bitcast.56, bf16[12,1536,128]{2,1,0:T(8,128)(2,1)} %param.7, s32[]{:T(128)S(6)} %select_n.6), kind=kOutput, calls=%fused_computation.15 | convolution fusion | flops 1207959552 | bytes 5898244 | tf_op jit(solution)/shard_map/td,cdn->ctn/dot_general | solution.py:47
  73.8 0.8 collective-permute-done
  74.6 0.0 copy-done.4
  74.6 2.7 %fusion.2 = bf16[6,1024,128]{1,2,0:T(8,128)(2,1)S(1)} fusion(bf16[6,1024,128]{1,2,0:T(8,128)(2,1)S(1)} %collective-permute-done, f32[6,128,1024]{2,1,0:T(8,128)S(1)} %fusion.8, bf16[1024,768,1]{1,0,2:T(8,128)(2,1)S(1)} %bitcast.61, bf16[12,1536,128]{2,1,0:T(8,128)(2,1)} %param.7, s32[]{:T(128)S(6)} %select_n.6, s32[]{:T(128)S(6)} %add.78), kind=kOutput, calls=%fused_computation.5 | convolution fusion | flops 1211105280 | bytes 9043976 | tf_op jit(solution)/shard_map/td,cdn->ctn/dot_general | solution.py:48
  77.3 1.3 copy.36
  78.7 0.0 copy-start.3
  78.7 4.4 %all-to-all-start.3 = ((bf16[4,6,256,128]{2,3,1,0:T(8,128)(2,1)}), bf16[4,6,256,128]{2,3,1,0:T(8,128)(2,1)S(1)}, u32[]{:S(2)}, u32[]{:S(2)}) async-start(bf16[4,6,256,128]{2,3,1,0:T(8,128)(2,1)} %bitcast.45), calls=%async_computation.3 | async-start | bytes 3145728 | tf_op jit(solution)/shard_map/all_to_all | solution.py:18
  83.1 0.0 reduce-scatter.2.cloned.1.call-start
  83.1 0.0 copy-done
  83.1 0.1 compare_reduce_fusion
  83.2 0.0 copy-done.3
  83.3 20.8 %all-to-all-done.3 = bf16[4,6,256,128]{2,3,1,0:T(8,128)(2,1)S(1)} async-done(((bf16[4,6,256,128]{2,3,1,0:T(8,128)(2,1)}), bf16[4,6,256,128]{2,3,1,0:T(8,128)(2,1)S(1)}, u32[]{:S(2)}, u32[]{:S(2)}) %all-to-all-start.3) | async-done | bytes 1572896 | tf_op jit(solution)/shard_map/all_to_all | solution.py:18
  104.1 0.0 slice-start
  104.1 0.2 convert_reduce_fusion
  104.3 0.2 multiply_convert_fusion
  104.5 0.2 copy.23
  104.7 0.0 slice-start.1
  104.7 0.3 broadcast_in_dim.11
  105.1 22.8 %all_to_all.42 = bf16[4,6,256,128]{3,2,1,0:T(8,128)(2,1)S(1)} all-to-all(bf16[4,6,256,128]{3,2,1,0:T(8,128)(2,1)S(1)} %broadcast_in_dim.11), channel_id=1, replica_groups=mesh['x'=4,'core'=2,'z'=8,'y'=4] {'x'}, dimensions={0} | all-to-all | bytes 3145728 | tf_op jit(solution)/shard_map/all_to_all | solution.py:12
  127.9 0.1 copy.24
  128.1 0.0 copy-start.2
  128.1 0.3 collective-permute-start.1
  128.4 0.0 slice-done
  128.4 0.0 slice-done.1
  128.4 1.7 fusion.24
  130.1 0.0 copy-done.2
  130.1 1.4 fusion.11
  131.5 0.2 collective-permute-done.1
  131.8 0.0 copy-start.5
  131.8 1.2 copy-done.5
  132.9 0.0 copy-start.1
  132.9 3.0 %fusion = bf16[1024,768]{1,0:T(8,128)(2,1)} fusion(f32[1024,768,1]{1,0,2:T(8,128)S(1)} %fusion.11, bf16[6,1024,128]{2,1,0:T(8,128)(2,1)S(1)} %collective-permute-done.1, bf16[12,128,768]{2,1,0:T(8,128)(2,1)S(1)} %get-tuple-element.10, s32[]{:T(128)S(6)} %select_n.7), kind=kOutput, calls=%fused_computation.1 | convolution fusion | flops 1209532416 | bytes 7471108 | tf_op jit(solution)/shard_map/ctn,cnd->td/dot_general | solution.py:71
  135.9 0.0 reduce-scatter.2.cloned.1.call-update
  135.9 0.0 copy-done.1
  135.9 0.0 copy-start.6
  136.0 2.9 %fusion.14 = f32[1024,768,1]{1,0,2:T(8,128)S(1)} fusion(bf16[6,1024,128]{2,1,0:T(8,128)(2,1)} %bitcast.54, bf16[12,128,768]{2,1,0:T(8,128)(2,1)S(1)} %copy-done.1, s32[]{:T(128)S(6)} %select_n.6), kind=kOutput, calls=%fused_computation.21 | convolution fusion | flops 1207959552 | bytes 5898244 | tf_op jit(solution)/shard_map/ctn,cnd->td/dot_general | solution.py:70
  138.9 0.0 copy-done.6
  138.9 1.4 fusion.1
  140.3 0.1 copy.37
  140.5 23.9 %all_to_all.43 = bf16[4,8,32,768]{3,2,1,0:T(8,128)(2,1)S(1)} all-to-all(bf16[4,8,32,768]{3,2,1,0:T(8,128)(2,1)S(1)} %bitcast.49), channel_id=1, replica_groups=mesh['x'=4,'core'=2,'z'=8,'y'=4] {'y'}, dimensions={0} | all-to-all | bytes 3145728 | tf_op jit(solution)/shard_map/all_to_all | solution.py:18
  164.3 0.3 reduce_sum.46
  164.6 17.6 %all_to_all.44 = bf16[8,32,768]{2,1,0:T(8,128)(2,1)S(1)} all-to-all(bf16[8,32,768]{2,1,0:T(8,128)(2,1)S(1)} %reduce_sum.46), channel_id=1, replica_groups=mesh['x'=4,'core'=2,'z'=8,'y'=4] {'z'}, dimensions={0} | all-to-all | bytes 786432 | tf_op jit(solution)/shard_map/all_to_all | solution.py:18
  182.2 0.0 reduce-scatter.2.cloned.1.call-done
  182.2 5.0 %all-to-all-start.7 = ((bf16[4,32,768]{2,1,0:T(8,128)(2,1)}), bf16[4,32,768]{2,1,0:T(8,128)(2,1)S(1)}, u32[]{:S(2)}, u32[]{:S(2)}) async-start(bf16[4,32,768]{2,1,0:T(8,128)(2,1)} %bitcast.59), calls=%async_computation.8 | async-start | bytes 393216 | tf_op jit(solution)/shard_map/all_to_all | solution.py:18
  187.2 0.1 reduce_sum.47
  187.3 4.8 %all-to-all-done.7 = bf16[4,32,768]{2,1,0:T(8,128)(2,1)S(1)} async-done(((bf16[4,32,768]{2,1,0:T(8,128)(2,1)}), bf16[4,32,768]{2,1,0:T(8,128)(2,1)S(1)}, u32[]{:S(2)}, u32[]{:S(2)}) %all-to-all-start.7) | async-done | bytes 196640 | tf_op jit(solution)/shard_map/all_to_all | solution.py:18
  192.1 0.6 pad_maximum_fusion
  (8 shorter events, 0.1 us)
Async XLA Ops:
  6.5 76.5 %copy-start = (s32[1024,48]{0,1:T(8,128)S(1)}, s32[1024,48]{0,1:T(8,128)}, u32[]{:S(2)}) copy-start(s32[1024,48]{0,1:T(8,128)} %param.6) | copy-start | bytes 589828
  6.5 59.1 %all-gather.3.cloned.1.call-start = ((), (), s32[]{:S(2)}) async-start(), calls=%async_computation.10 | async-start | bytes 1769472 | tf_op jit(solution)/shard_map/all_gather | solution.py:41
  41.9 19.2 %all-to-all-start.2 = ((bf16[4,8,32,768]{3,2,1,0:T(8,128)(2,1)}), bf16[4,8,32,768]{3,2,1,0:T(8,128)(2,1)S(1)}, u32[]{:S(2)}, u32[]{:S(2)}) async-start(bf16[4,8,32,768]{3,2,1,0:T(8,128)(2,1)} %broadcast_in_dim.10), calls=%async_computation.2 | async-start | bytes 3145728 | tf_op jit(solution)/shard_map/all_to_all | solution.py:12
  71.0 3.6 %collective-permute-start = (bf16[6,1024,128]{1,2,0:T(8,128)(2,1)}, bf16[6,1024,128]{1,2,0:T(8,128)(2,1)S(1)}, u32[]{:S(2)}, u32[]{:S(2)}) collective-permute-start(bf16[6,1024,128]{1,2,0:T(8,128)(2,1)} %fusion.3), channel_id=1, source_target_pairs={{0,32},{32,0},{1,33},{33,1},{2,34},{34,2},{3,35},{35,3},{4,36},{36... | collective-permute-start | bytes 4718600 | tf_op jit(solution)/shard_map/ppermute | solution.py:26
  71.0 3.6 %copy-start.4 = (bf16[32,32,768]{2,1,0:T(8,128)(2,1)S(1)}, bf16[32,32,768]{2,1,0:T(8,128)(2,1)}, u32[]{:S(2)}) copy-start(bf16[32,32,768]{2,1,0:T(8,128)(2,1)} %all-gather.3.cloned.1.call-done) | copy-start | bytes 4718596
  78.7 4.6 %copy-start.3 = (f32[12,128]{1,0:T(8,128)S(1)}, f32[12,128]{1,0:T(8,128)}, u32[]{:S(2)}) copy-start(f32[12,128]{1,0:T(8,128)} %param.8) | copy-start | bytes 18436
  78.7 25.4 %all-to-all-start.3 = ((bf16[4,6,256,128]{2,3,1,0:T(8,128)(2,1)}), bf16[4,6,256,128]{2,3,1,0:T(8,128)(2,1)S(1)}, u32[]{:S(2)}, u32[]{:S(2)}) async-start(bf16[4,6,256,128]{2,3,1,0:T(8,128)(2,1)} %bitcast.45), calls=%async_computation.3 | async-start | bytes 3145728 | tf_op jit(solution)/shard_map/all_to_all | solution.py:18
  83.1 99.2 %reduce-scatter.2.cloned.1.call-start = ((), (), s32[]{:S(2)}) async-start(), calls=%async_computation.9 | async-start | bytes 1769472 | tf_op jit(solution)/shard_map/reduce_scatter | solution.py:75
  104.1 24.3 %slice-start = ((s8[4718592]{0:T(1024)(128)(4,1)}), s8[524288]{0:T(1024)(128)(4,1)S(1)}, s32[]{:S(2)}) async-start(s8[4718592]{0:T(1024)(128)(4,1)} %bitcast.50), calls=%async_computation.11 | async-start | bytes 1048576
  104.7 23.7 %slice-start.1 = ((s8[4718592]{0:T(1024)(128)(4,1)}), s8[4194304]{0:T(1024)(128)(4,1)S(1)}, s32[]{:S(2)}) async-start(s8[4718592]{0:T(1024)(128)(4,1)} %bitcast.50), calls=%async_computation.12 | async-start | bytes 8388608
  128.1 2.1 %copy-start.2 = (bf16[6,4,256,128]{3,2,1,0:T(8,128)(2,1)}, bf16[6,4,256,128]{3,2,1,0:T(8,128)(2,1)S(1)}, u32[]{:S(2)}) copy-start(bf16[6,4,256,128]{3,2,1,0:T(8,128)(2,1)S(1)} %copy.24) | copy-start | bytes 4718596
  128.1 3.7 %collective-permute-start.1 = (bf16[6,1024,128]{2,1,0:T(8,128)(2,1)S(1)}, bf16[6,1024,128]{2,1,0:T(8,128)(2,1)S(1)}, u32[]{:S(2)}, u32[]{:S(2)}) collective-permute-start(bf16[6,1024,128]{2,1,0:T(8,128)(2,1)S(1)} %bitcast.52), channel_id=1, source_target_pairs={{0,32},{32,0},{1,33},{33,1},{2,34},{34,2},{3,35},{35,3},{4,36},{36... | collective-permute-start | bytes 4718600 | tf_op jit(solution)/shard_map/ppermute | solution.py:26
  131.8 1.2 copy-start.5
  132.9 3.0 %copy-start.1 = (bf16[12,128,768]{2,1,0:T(8,128)(2,1)S(1)}, bf16[12,128,768]{2,1,0:T(8,128)(2,1)}, u32[]{:S(2)}) copy-start(bf16[12,128,768]{2,1,0:T(8,128)(2,1)} %get-tuple-element.9) | copy-start | bytes 7077892
  135.9 2.9 %copy-start.6 = (bf16[6,1024,128]{2,1,0:T(8,128)(2,1)S(1)}, bf16[6,1024,128]{2,1,0:T(8,128)(2,1)}, u32[]{:S(2)}) copy-start(bf16[6,1024,128]{2,1,0:T(8,128)(2,1)} %copy-done.5) | copy-start | bytes 4718596
  182.2 9.9 %all-to-all-start.7 = ((bf16[4,32,768]{2,1,0:T(8,128)(2,1)}), bf16[4,32,768]{2,1,0:T(8,128)(2,1)S(1)}, u32[]{:S(2)}, u32[]{:S(2)}) async-start(bf16[4,32,768]{2,1,0:T(8,128)(2,1)} %bitcast.59), calls=%async_computation.8 | async-start | bytes 393216 | tf_op jit(solution)/shard_map/all_to_all | solution.py:18
Sparse Core Ops, SparseCore 0:
  17.7 42.6 all-gather.2
  136.1 35.6 reduce-scatter.1

commit v2 on v1

v2 whole, which is shorter than its diff:
```python
import functools

import jax
import jax.numpy as jnp
from jax import lax
from jax.experimental import pallas as pl
from jax.experimental.pallas import tpu as pltpu
from jax.sharding import Mesh
from jax.sharding import PartitionSpec as P

F32, BF16, I32 = jnp.float32, jnp.bfloat16, jnp.int32
NX, NC, NZ, NY = 4, 2, 8, 4
SLOTS = 384
TILE = 256


def spread(block, axis):
    peers = lax.axis_size(axis)
    return lax.all_to_all(
        jnp.broadcast_to(block[None], (peers,) + block.shape), axis, split_axis=0, concat_axis=0
    )


def exchange(blocks, axis):
    return lax.all_to_all(blocks, axis, split_axis=0, concat_axis=0)


def total(blocks):
    return jnp.sum(blocks.astype(F32), axis=0)


def from_peer(block, axis, step):
    n = lax.axis_size(axis)
    return lax.ppermute(block, axis, [((i + step) % n, i) for i in range(n)])


def up_kernel(at_ref, xa_ref, xb_ref, w_ref, bias_ref, pos_ref, out_ref, xs, w2, acc):
    cut = xa_ref.shape[-1]
    rows = xa_ref.shape[-2]
    blocks = acc.shape[0]
    span = xs.shape[0] // blocks
    neurons = w_ref.shape[-1]

    @pl.when(pl.program_id(0) == 0)
    def _():
        for z in range(NZ):
            for y in range(NY):
                xs[(z * NY + y) * rows : (z * NY + y + 1) * rows, :cut] = xa_ref[y, z]
                to = (z * NY + lax.rem(at_ref[blocks] + y, NY)) * rows
                xs[pl.ds(pl.multiple_of(to, rows), rows), cut:] = xb_ref[z, y]
        acc[...] = jnp.zeros_like(acc)

    w2[:, :neurons] = w_ref[0]
    w2[:, neurons:] = w_ref[1]
    bias = jnp.concatenate([bias_ref[0, :1], bias_ref[0, 1:]], axis=1)
    slot = lax.broadcasted_iota(I32, (SLOTS, span), 0)

    @pl.loop(0, xs.shape[0] // TILE)
    def _(m):
        pre = jnp.dot(
            xs[pl.ds(pl.multiple_of(m * TILE, TILE), TILE)], w2[...], preferred_element_type=F32
        )
        pre = (pre + bias).astype(BF16)
        for h in range(TILE // span):
            b = m * (TILE // span) + h
            part = pre[h * span : (h + 1) * span]
            both = jnp.concatenate([part[:, :neurons], part[:, neurons:]], axis=0)
            take = jnp.concatenate(
                [
                    jnp.where(slot == pos_ref[0, pl.ds(b, 1), :], 1.0, 0.0),
                    jnp.where(slot == pos_ref[0, pl.ds(blocks + b, 1), :], 1.0, 0.0),
                ],
                axis=1,
            ).astype(BF16)
            acc[b] += jnp.dot(take, both, preferred_element_type=F32)

    @pl.when(pl.program_id(0) == pl.num_programs(0) - 1)
    def _():
        for j in range(blocks):
            out_ref[j] = acc[at_ref[j]].astype(BF16)


def packed_up(at, x_a, x_b, up_weight, bias, pos):
    clusters, width, neurons = up_weight.shape
    tokens = x_a.shape[0] * x_a.shape[1] * x_a.shape[2]
    blocks = NX * NC
    whole = lambda *shape: pl.BlockSpec(shape, lambda i, at: (0,) * len(shape))
    return pl.pallas_call(
        up_kernel,
        grid_spec=pltpu.PrefetchScalarGridSpec(
            num_scalar_prefetch=1,
            grid=(clusters // 2,),
            in_specs=[
                whole(*x_a.shape),
                whole(*x_b.shape),
                pl.BlockSpec((2, width, neurons), lambda i, at: (i, 0, 0)),
                pl.BlockSpec((1, 2, neurons), lambda i, at: (i, 0, 0)),
                pl.BlockSpec((1, 2 * blocks, tokens // blocks), lambda i, at: (i, 0, 0)),
            ],
            out_specs=whole(blocks, SLOTS, neurons),
            scratch_shapes=[
                pltpu.VMEM((tokens, width), BF16),
                pltpu.VMEM((width, 2 * neurons), BF16),
                pltpu.VMEM((blocks, SLOTS, neurons), F32),
            ],
        ),
        out_shape=jax.ShapeDtypeStruct((blocks, SLOTS, neurons), BF16),
        compiler_params=pltpu.CompilerParams(vmem_limit_bytes=32 << 20),
        cost_estimate=pl.CostEstimate(
            flops=2 * tokens * width * clusters * neurons, bytes_accessed=9 << 20, transcendentals=0
        ),
    )(at, x_a, x_b, up_weight, bias, pos)


def unpack_kernel(at_ref, packed_ref, pos_ref, out_ref):
    span, clusters = pos_ref.shape[1:]
    neurons = packed_ref.shape[-1]
    slot = lax.broadcasted_iota(I32, (span, SLOTS), 1)
    for c in range(0, clusters, 2):
        take = jnp.concatenate(
            [jnp.where(slot == pos_ref[0, :, k : k + 1], 1.0, 0.0) for k in (c, c + 1)], axis=0
        ).astype(BF16)
        both = jnp.dot(take, packed_ref[0], preferred_element_type=F32).astype(BF16)
        out_ref[:, c * neurons : (c + 1) * neurons] = both[:span]
        out_ref[:, (c + 1) * neurons : (c + 2) * neurons] = both[span:]


def unpack(at, packed, pos):
    blocks, span, clusters = pos.shape
    neurons = packed.shape[-1]
    return pl.pallas_call(
        unpack_kernel,
        grid_spec=pltpu.PrefetchScalarGridSpec(
            num_scalar_prefetch=1,
            grid=(blocks,),
            in_specs=[
                pl.BlockSpec((1, SLOTS, neurons), lambda j, at: (j, 0, 0)),
                pl.BlockSpec((1, span, clusters), lambda j, at: (at[j], 0, 0)),
            ],
            out_specs=pl.BlockSpec((span, clusters * neurons), lambda j, at: (at[j], 0)),
        ),
        out_shape=jax.ShapeDtypeStruct((blocks * span, clusters * neurons), BF16),
        compiler_params=pltpu.CompilerParams(vmem_limit_bytes=16 << 20),
        cost_estimate=pl.CostEstimate(
            flops=2 * blocks * span * SLOTS * clusters * neurons, bytes_accessed=4 << 20, transcendentals=0
        ),
    )(at, packed, pos)


def down_kernel(y_first, at_ref, hidden_ref, w_ref, out_ref):
    rows = out_ref.shape[-2]
    span = rows * NY
    wide = w_ref[...].reshape(-1, w_ref.shape[-1])

    @pl.loop(0, hidden_ref.shape[0] // TILE)
    def _(m):
        val = jnp.dot(
            hidden_ref[pl.ds(pl.multiple_of(m * TILE, TILE), TILE)], wide, preferred_element_type=F32
        ).astype(BF16)
        for h in range(TILE // span):
            z = m * (TILE // span) + h
            for y in range(NY):
                piece = val[h * span + y * rows : h * span + (y + 1) * rows]
                if y_first:
                    out_ref[y, z] = piece
                else:
                    out_ref[z, lax.rem(y + NY - at_ref[NX * NC], NY)] = piece


def down(at, hidden, down_weight, low, high, y_first):
    tokens, inner = hidden.shape
    clusters, neurons, _ = down_weight.shape
    rows = tokens // (NY * NZ)
    lead = (NY, NZ) if y_first else (NZ, NY)
    return pl.pallas_call(
        functools.partial(down_kernel, y_first),
        grid_spec=pltpu.PrefetchScalarGridSpec(
            num_scalar_prefetch=1,
            grid=((high - low) // TILE,),
            in_specs=[
                pl.BlockSpec((tokens, inner), lambda n, at: (0, 0)),
                pl.BlockSpec((clusters, neurons, TILE), lambda n, at: (0, 0, n + low // TILE)),
            ],
            out_specs=pl.BlockSpec(lead + (rows, TILE), lambda n, at: (0, 0, 0, n)),
        ),
        out_shape=jax.ShapeDtypeStruct(lead + (rows, high - low), BF16),
        compiler_params=pltpu.CompilerParams(vmem_limit_bytes=32 << 20),
        cost_estimate=pl.CostEstimate(
            flops=2 * tokens * inner * (high - low), bytes_accessed=7 << 20, transcendentals=0
        ),
    )(at, hidden, down_weight)


def on_device(activations, picks, up_weight, up_bias, down_weight):
    rows, width = activations.shape
    clusters, _, neurons = up_weight.shape
    tokens = NZ * NY * rows
    blocks = NX * NC
    span = tokens // blocks
    cut = width // 2
    core, xi = lax.axis_index("core"), lax.axis_index("x")
    zi, yi = lax.axis_index("z"), lax.axis_index("y")

    first, second = activations[:, :cut], activations[:, cut:]
    near = jnp.stack([second] + [from_peer(second, "y", k) for k in range(1, NY)])
    x_b = lax.all_gather(near, "z", axis=0)
    x_a = spread(spread(first, "z"), "y")

    wanted = (zi * NY + yi) * clusters + jnp.arange(clusters, dtype=I32)
    mask = jnp.any(picks[:, :, None] == wanted[None, None, :], axis=1)
    hits = mask.reshape(blocks, span, clusters).astype(BF16)
    before = jnp.tril(jnp.ones((span, span), BF16), -1)
    ahead = jnp.triu(jnp.ones((clusters, clusters), BF16), 1)
    each = jnp.sum(hits, axis=2).astype(BF16)
    base = jnp.einsum("bt,st->bs", each, before, preferred_element_type=F32)
    within = jnp.einsum("btk,kc->btc", hits, ahead, preferred_element_type=F32)
    pos = jnp.where(hits > 0, base[:, :, None] + within, -1.0).astype(I32)
    groups = picks.reshape(blocks, span, -1) // clusters
    load = jnp.sum(
        (groups[:, :, :, None] == jnp.arange(NZ * NY, dtype=I32)).astype(I32), axis=(1, 2)
    )
    fits = jnp.max(load) <= SLOTS

    order = [((core + j // NX) % NC) * NX + (xi + j % NX) % NX for j in range(blocks)]
    at = jnp.stack([*order, yi]).astype(I32)

    def packed(x_a, x_b, pos):
        by_pair = pos.transpose(2, 0, 1).reshape(clusters // 2, 2 * blocks, span)
        bias = (up_bias * (1.0 / blocks)).reshape(clusters // 2, 2, neurons)
        part = packed_up(at, x_a, x_b, up_weight, bias, by_pair)
        part = part[:NX].astype(F32) + from_peer(part[NX:], "core", 1).astype(F32)
        summed = part[0]
        part = part.astype(BF16)
        for k in range(1, NX):
            summed = summed + from_peer(part[k], "x", -k).astype(F32)
        own = jnp.maximum(summed, 0.0).astype(BF16)
        own = jnp.stack([own] + [from_peer(own, "x", k) for k in range(1, NX)])
        both = jnp.concatenate([own, from_peer(own, "core", 1)], axis=0)
        return unpack(at, both, pos)

    def dense(x_a, x_b, pos):
        x_0 = x_a.transpose(1, 0, 2, 3).reshape(tokens, cut)
        x_1 = jnp.roll(x_b, yi, axis=1).reshape(tokens, width - cut)
        part = jnp.einsum("td,cdn->tcn", x_0, up_weight[:, :cut], preferred_element_type=F32)
        part += jnp.einsum("td,cdn->tcn", x_1, up_weight[:, cut:], preferred_element_type=F32)
        part = part.astype(BF16).reshape(blocks, span, clusters, neurons)
        summed = total(exchange(part, ("x", "core"))) + up_bias[None]
        keep = lax.dynamic_index_in_dim(pos, xi * NC + core, 0, keepdims=False) >= 0
        own = jnp.where(keep[:, :, None], jnp.maximum(summed, 0.0), 0.0).astype(BF16)
        return spread(own, ("x", "core")).reshape(tokens, clusters * neurons)

    hidden = lax.cond(fits, packed, dense, x_a, x_b, pos)

    out_b = down(at, hidden, down_weight, cut, width, False)
    out_b = lax.psum_scatter(out_b, "z", scatter_dimension=0)
    out_a = down(at, hidden, down_weight, 0, cut, True)
    out_a = total(exchange(out_a, "y")).astype(BF16)
    out_a = total(exchange(out_a, "z")).astype(BF16)
    done = out_b[0].astype(F32)
    for k in range(1, NY):
        done = done + from_peer(out_b[k], "y", -k).astype(F32)
    return jnp.concatenate([out_a, done.astype(BF16)], axis=1)


def solution(mesh):
    grid = Mesh(mesh.devices.reshape(NX, NC, NZ, NY), ("x", "core", "z", "y"))
    dp, clus = ("x", "core"), ("z", "y")
    placed = (P(clus, dp), P(), P(clus, dp, None), P(clus, None), P(clus, None, dp))
    return jax.shard_map(
        on_device, mesh=grid, in_specs=placed, out_specs=P(clus, dp), check_vma=False
    )
```

time: 200 us -> 185 us (0.925)
  blocking collectives: 97.4 us -> 23.7 us
  Pallas kernels: 0 us -> 41 us
  starting transfers between devices: 15.7 us -> 40.2 us
  matrix products: 23.9 us -> 0.36 us
  waiting for transfers between devices: 39.9 us -> 47.3 us
  other arithmetic: 1.59 us -> 6.75 us
  local copies, waits for them, and re-layouts: 7.47 us -> 10.8 us
    all_to_all x3 -> x0, blocking collectives: 56 us -> none  [spread(): lax.all_to_all(jnp.broadcast_to(block[None], (peers,) + block.shape), axi...]
    pallas_call x0 -> x4, Pallas kernels: none -> 41 us  [the longest x1 22.2 us: packed_up(): pl.pallas_call(up_kernel, grid_spec=pltpu.PrefetchScalarGridSpec(num_scal...]
    dot_general x8 -> x2, matrix products: 23.9 us -> 0.36 us  [the longest x1 0.2 us: on_device(): base = jnp.einsum('bt,st->bs', each, before, preferred_element_type=F32)]
    ppermute x2 -> x14, starting transfers between devices: 0.28 us -> 19.5 us  [from_peer(): return lax.ppermute(block, axis, [((i + step) % n, i) for i in range(n)])]
    all_to_all x2 -> x1, blocking collectives: 41.4 us -> 23.7 us  [exchange(): return lax.all_to_all(blocks, axis, split_axis=0, concat_axis=0)]
    all_to_all x2 -> x1, waiting for transfers between devices: 25.6 us -> 9.11 us  [exchange(): return lax.all_to_all(blocks, axis, split_axis=0, concat_axis=0)]
    ppermute x2 -> x14, waiting for transfers between devices: 1.03 us -> 14.9 us  [from_peer(): return lax.ppermute(block, axis, [((i + step) % n, i) for i in range(n)])]
    all_to_all x1 -> x2, starting transfers between devices: 6.02 us -> 16.7 us  [spread(): lax.all_to_all(jnp.broadcast_to(block[None], (peers,) + block.shape), axi...]
  transfers between devices with their start and end apart: 7 -> 19, of which waited for: 5 -> 11; matrix products, arithmetic and copies ran while one was open for 8% -> 4% of each run, Pallas kernels for 0% -> 3%
where the time goes in v2:
time: 185 us
  waiting for transfers between devices  47.3 us (26%)
  Pallas kernels  41 us (22%)
  starting transfers between devices  40.2 us (22%)
  blocking collectives  23.7 us (13%)
  between operations  14.3 us (8%)
  local copies, waits for them, and re-layouts  10.8 us (6%)
  other arithmetic  6.75 us (4%)
    all_to_all x1, blocking collectives, exchange(): return lax.all_to_all(blocks, axis, split_axis=0, concat_axis=0)  23.7 us
    all_to_all x2, waiting for transfers between devices, spread(): lax.all_to_all(jnp.broadcast_to(block[None], (peers,) + block.shape), axi...  23.3 us
    pallas_call x1, Pallas kernels, packed_up(): pl.pallas_call(up_kernel, grid_spec=pltpu.PrefetchScalarGridSpec(num_scal...  22.2 us
    ppermute x14, starting transfers between devices, from_peer(): return lax.ppermute(block, axis, [((i + step) % n, i) for i in range(n)])  19.5 us
    all_to_all x2, starting transfers between devices, spread(): lax.all_to_all(jnp.broadcast_to(block[None], (peers,) + block.shape), axi...  16.7 us
    ppermute x14, waiting for transfers between devices, from_peer(): return lax.ppermute(block, axis, [((i + step) % n, i) for i in range(n)])  14.9 us
    pallas_call x2, Pallas kernels, down(): pl.pallas_call(functools.partial(down_kernel, y_first), grid_spec=pltpu.P...  14 us
    all_to_all x1, waiting for transfers between devices, exchange(): return lax.all_to_all(blocks, axis, split_axis=0, concat_axis=0)  9.11 us
  transfers between devices with their start and end apart: 19, of which 11 were waited for; matrix products, arithmetic and copies ran while one was open for 4% of the time, Pallas kernels for 3%

profile of v2, /device:TPU:8, one launch (start us, length us, event | category | flops | bytes accessed | tf_op | source)
XLA Modules:
  0.0 184.6 jit_solution(2787039679981767192)
XLA Ops:
  6.5 0.9 slice_bitcast_fusion.9
  7.4 2.3 %collective-permute-start.8 = (bf16[32,768]{1,0:T(8,128)(2,1)S(1)}, bf16[32,768]{1,0:T(8,128)(2,1)S(1)}, u32[]{:S(2)}, u32[]{:S(2)}) collective-permute-start(bf16[32,768]{1,0:T(8,128)(2,1)S(1)} %get-tuple-element.132), channel_id=1, source_target_pairs={{1,0},{2,1},{3,2},{0,3},{5,4},{6,5},{7,6},{4,7},{9,8},{10,9},{11,1... | collective-permute-start | bytes 147464 | tf_op jit(solution)/shard_map/ppermute | solution.py:34
  9.7 0.9 collective-permute-start.9
  10.5 1.9 %collective-permute-start.10 = (bf16[32,768]{1,0:T(8,128)(2,1)S(1)}, bf16[32,768]{1,0:T(8,128)(2,1)S(1)}, u32[]{:S(2)}, u32[]{:S(2)}) collective-permute-start(bf16[32,768]{1,0:T(8,128)(2,1)S(1)} %get-tuple-element.132), channel_id=1, source_target_pairs={{3,0},{0,1},{1,2},{2,3},{7,4},{4,5},{5,6},{6,7},{11,8},{8,9},{9,10... | collective-permute-start | bytes 147464 | tf_op jit(solution)/shard_map/ppermute | solution.py:34
  12.4 2.8 %collective-permute-done.9 = bf16[32,768]{1,0:T(8,128)(2,1)S(1)} collective-permute-done((bf16[32,768]{1,0:T(8,128)(2,1)S(1)}, bf16[32,768]{1,0:T(8,128)(2,1)S(1)}, u32[]{:S(2)}, u32[]{:S(2)}) %collective-permute-start.9) | collective-permute-done | bytes 49184 | tf_op jit(solution)/shard_map/ppermute | solution.py:34
  15.3 0.7 pad_maximum_fusion.1
  16.0 0.0 all-gather.3.cloned.1.call-update
  16.0 0.8 broadcast_in_dim.58
  16.8 7.8 %all-to-all-start.2 = ((bf16[8,32,768]{2,1,0:T(8,128)(2,1)}), bf16[8,32,768]{2,1,0:T(8,128)(2,1)S(1)}, u32[]{:S(2)}, u32[]{:S(2)}) async-start(bf16[8,32,768]{2,1,0:T(8,128)(2,1)} %broadcast_in_dim.58), calls=%async_computation.2 | async-start | bytes 786432 | tf_op jit(solution)/shard_map/all_to_all | solution.py:19
  24.6 1.0 divide_bitcast_fusion
  25.7 0.1 fusion.17
  25.9 0.0 copy-start.6
  25.9 13.4 %all-to-all-done.2 = bf16[8,32,768]{2,1,0:T(8,128)(2,1)S(1)} async-done(((bf16[8,32,768]{2,1,0:T(8,128)(2,1)}), bf16[8,32,768]{2,1,0:T(8,128)(2,1)S(1)}, u32[]{:S(2)}, u32[]{:S(2)}) %all-to-all-start.2) | async-done | bytes 393248 | tf_op jit(solution)/shard_map/all_to_all | solution.py:19
  39.3 1.3 broadcast_in_dim.59
  40.7 8.8 %all-to-all-start.3 = ((bf16[4,8,32,768]{3,2,1,0:T(8,128)(2,1)}), bf16[4,8,32,768]{3,2,1,0:T(8,128)(2,1)}, u32[]{:S(2)}, u32[]{:S(2)}) async-start(bf16[4,8,32,768]{3,2,1,0:T(8,128)(2,1)} %broadcast_in_dim.59), calls=%async_computation.3 | async-start | bytes 3145728 | tf_op jit(solution)/shard_map/all_to_all | solution.py:19
  49.5 0.4 compare_reduce_fusion
  50.0 0.9 convert_reduce_fusion.1
  50.9 0.7 reduce_max.9
  52.3 0.1 stack.69.at_ref
  52.4 0.2 fusion.23
  52.6 0.2 fusion.15
  52.8 9.9 %all-to-all-done.3 = bf16[4,8,32,768]{3,2,1,0:T(8,128)(2,1)} async-done(((bf16[4,8,32,768]{3,2,1,0:T(8,128)(2,1)}), bf16[4,8,32,768]{3,2,1,0:T(8,128)(2,1)}, u32[]{:S(2)}, u32[]{:S(2)}) %all-to-all-start.3) | async-done | bytes 1572896 | tf_op jit(solution)/shard_map/all_to_all | solution.py:19
  62.7 50.1 %conditional.1 = (bf16[1024,1536]{1,0:T(8,128)(2,1)S(1)}) conditional(s32[]{:T(128)} %convert_element_type.74, (s32[]{:T(128)}, s32[]{:T(128)}, s32[8,128,12]{1,2,0:T(8,128)S(1)}, bf16[4,8,32,768]{3,2,1,0:T(8,128)(2,1)}, bf16[12,1536,128]{2,1,0:T(8,128)(2,1)}, /*index=5*/bf16[8,4,32,768]{3,2,1,0:T(8,128)(2,1)}, s32[]{:T(128)}, ...), branch_computations={%region_4.6_spmd, %region_6.7_spmd} | conditional | flops 6041568768 | bytes 94387544 | solution.py:252
  62.8 22.2 %branch_1_fun.2 = bf16[8,384,128]{2,1,0:T(8,128)(2,1)S(1)} custom-call(s32[9]{0:T(128)S(1)} %get-tuple-element.44.at_ref, bf16[4,8,32,768]{3,2,1,0:T(8,128)(2,1)} %get-tuple-element.45.xa_ref, bf16[8,4,32,768]{3,2,1,0:T(8,128)(2,1)} %get-tuple-element.46.xb_ref, bf16[12,1536,128]{2,1,0:T(8,128)(2,1)} %get-tuple-element.47.w_ref, ...), custom_call_target="tpu_custom_call" | custom-call | flops 4831838208 | bytes 9437184 | tf_op jit(solution)/shard_map/cond/branch_1_fun/pallas_call | solution.py:88
  85.1 0.1 collective-permute-start
  85.2 1.7 collective-permute-done
  86.9 0.1 convert_add_fusion
  87.0 1.8 collective-permute-start.1
  88.8 2.7 %collective-permute-start.2 = (bf16[384,128]{1,0:T(8,128)(2,1)S(1)}, bf16[384,128]{1,0:T(8,128)(2,1)S(1)}, u32[]{:S(2)}, u32[]{:S(2)}) collective-permute-start(bf16[384,128]{1,0:T(8,128)(2,1)S(1)} %get-tuple-element.127), channel_id=1, source_target_pairs={{128,0},{192,64},{0,128},{64,192},{129,1},{193,65},{1,129},{65,193... | collective-permute-start | bytes 294920 | tf_op jit(solution)/shard_map/cond/branch_1_fun/ppermute | solution.py:34
  91.5 1.5 collective-permute-start.3
  92.9 0.2 collective-permute-done.1
  93.1 3.2 %collective-permute-done.2 = bf16[384,128]{1,0:T(8,128)(2,1)S(1)} collective-permute-done((bf16[384,128]{1,0:T(8,128)(2,1)S(1)}, bf16[384,128]{1,0:T(8,128)(2,1)S(1)}, u32[]{:S(2)}, u32[]{:S(2)}) %collective-permute-start.2) | collective-permute-done | bytes 98336 | tf_op jit(solution)/shard_map/cond/branch_1_fun/ppermute | solution.py:34
  96.4 0.1 constant_dynamic-update-slice_fusion.4
  96.4 2.5 %collective-permute-start.4 = (bf16[384,128]{1,0:T(8,128)(2,1)S(1)}, bf16[384,128]{1,0:T(8,128)(2,1)S(1)}, u32[]{:S(2)}, u32[]{:S(2)}) collective-permute-start(bf16[384,128]{1,0:T(8,128)(2,1)S(1)} %get-tuple-element.122), channel_id=1, source_target_pairs={{64,0},{128,64},{192,128},{0,192},{65,1},{129,65},{193,129},{1,193... | collective-permute-start | bytes 294920 | tf_op jit(solution)/shard_map/cond/branch_1_fun/ppermute | solution.py:34
  98.9 0.9 collective-permute-start.5
  99.8 0.8 collective-permute-start.6
  100.6 0.2 copy.56.pos_ref
  100.8 0.9 collective-permute-done.4
  101.8 3.3 %collective-permute-done.5 = bf16[384,128]{1,0:T(8,128)(2,1)S(1)} collective-permute-done((bf16[384,128]{1,0:T(8,128)(2,1)S(1)}, bf16[384,128]{1,0:T(8,128)(2,1)S(1)}, u32[]{:S(2)}, u32[]{:S(2)}) %collective-permute-start.5) | collective-permute-done | bytes 98336 | tf_op jit(solution)/shard_map/cond/branch_1_fun/ppermute | solution.py:34
  105.1 1.0 collective-permute-done.6
  106.1 0.1 pad_maximum_fusion
  106.1 0.1 collective-permute-start.7
  106.3 1.6 collective-permute-done.7
  107.9 0.1 constant_dynamic-update-slice_fusion.packed_ref
  108.0 4.8 %branch_1_fun.3 = bf16[1024,1536]{1,0:T(8,128)(2,1)S(1)} custom-call(s32[9]{0:T(128)S(1)} %get-tuple-element.44.at_ref, bf16[8,384,128]{2,1,0:T(8,128)(2,1)S(1)} %constant_dynamic-update-slice_fusion.packed_ref, s32[8,128,12]{2,1,0:T(8,128)S(1)} %copy.56.pos_ref), custom_call_target="tpu_custom_call" | custom-call | flops 1207959552 | bytes 4194304 | tf_op jit(solution)/shard_map/cond/branch_1_fun/pallas_call | solution.py:131
  112.8 1.6 copy-done.2
  114.4 2.3 %copy-done = bf16[12,128,1536]{2,1,0:T(8,128)(2,1)S(1)} copy-done((bf16[12,128,1536]{2,1,0:T(8,128)(2,1)S(1)}, bf16[12,128,1536]{2,1,0:T(8,128)(2,1)}, u32[]{:S(2)}) %copy-start) | copy-done | bytes 4718616
  116.8 8.4 %shard_map.56 = bf16[8,4,32,768]{3,2,1,0:T(8,128)(2,1)} custom-call(s32[9]{0:T(128)S(1)} %stack.69.at_ref, bf16[1024,1536]{1,0:T(8,128)(2,1)} %copy-done.2, bf16[12,128,1536]{2,1,0:T(8,128)(2,1)S(1)} %copy-done), custom_call_target="tpu_custom_call" | custom-call | flops 2415919104 | bytes 7340032 | tf_op jit(solution)/shard_map/pallas_call | solution.py:175
  125.2 0.0 reduce-scatter.2.cloned.1.call-update
  125.2 0.0 copy-start.1
  125.2 2.3 %copy-done.1 = bf16[12,128,1536]{2,1,0:T(8,128)(2,1)S(1)} copy-done((bf16[12,128,1536]{2,1,0:T(8,128)(2,1)S(1)}, bf16[12,128,1536]{2,1,0:T(8,128)(2,1)}, u32[]{:S(2)}) %copy-start.1) | copy-done | bytes 4718616
  127.6 5.5 %shard_map.55 = bf16[4,8,32,768]{3,2,1,0:T(8,128)(2,1)S(1)} custom-call(s32[9]{0:T(128)S(1)} %stack.69.at_ref, bf16[1024,1536]{1,0:T(8,128)(2,1)S(1)} %copy-done.3, bf16[12,128,1536]{2,1,0:T(8,128)(2,1)S(1)} %copy-done.1), custom_call_target="tpu_custom_call" | custom-call | flops 2415919104 | bytes 7340032 | tf_op jit(solution)/shard_map/pallas_call | solution.py:175
  133.1 23.7 %all_to_all.29 = bf16[4,8,32,768]{3,2,1,0:T(8,128)(2,1)S(1)} all-to-all(bf16[4,8,32,768]{3,2,1,0:T(8,128)(2,1)S(1)} %shard_map.55), channel_id=1, replica_groups=mesh['x'=4,'core'=2,'z'=8,'y'=4] {'y'}, dimensions={0} | all-to-all | bytes 3145728 | tf_op jit(solution)/shard_map/all_to_all | solution.py:25
  156.8 1.1 reduce_sum.59
  158.0 4.0 %all-to-all-start.5 = ((bf16[8,32,768]{2,1,0:T(8,128)(2,1)}), bf16[8,32,768]{2,1,0:T(8,128)(2,1)S(1)}, u32[]{:S(2)}, u32[]{:S(2)}) async-start(bf16[8,32,768]{2,1,0:T(8,128)(2,1)} %reduce_sum.59), calls=%async_computation.5 | async-start | bytes 786432 | tf_op jit(solution)/shard_map/all_to_all | solution.py:25
  162.0 0.0 reduce-scatter.2.cloned.1.call-done
  162.0 0.9 slice_bitcast_fusion.6
  162.9 0.8 collective-permute-start.11
  163.7 2.8 %collective-permute-start.12 = (bf16[32,768]{1,0:T(8,128)(2,1)S(1)}, bf16[32,768]{1,0:T(8,128)(2,1)S(1)}, u32[]{:S(2)}, u32[]{:S(2)}) collective-permute-start(bf16[32,768]{1,0:T(8,128)(2,1)S(1)} %get-tuple-element.130), channel_id=1, source_target_pairs={{2,0},{3,1},{0,2},{1,3},{6,4},{7,5},{4,6},{5,7},{10,8},{11,9},{8,1... | collective-permute-start | bytes 147464 | tf_op jit(solution)/shard_map/ppermute | solution.py:34
  166.5 0.6 collective-permute-start.13
  167.0 9.1 %all-to-all-done.5 = bf16[8,32,768]{2,1,0:T(8,128)(2,1)S(1)} async-done(((bf16[8,32,768]{2,1,0:T(8,128)(2,1)}), bf16[8,32,768]{2,1,0:T(8,128)(2,1)S(1)}, u32[]{:S(2)}, u32[]{:S(2)}) %all-to-all-start.5) | async-done | bytes 393248 | tf_op jit(solution)/shard_map/all_to_all | solution.py:25
  176.2 0.1 reduce_sum.60
  176.2 0.8 fusion.20
  177.1 0.6 pad_maximum_fusion.2
  (33 shorter events, 0.4 us)
Async XLA Ops:
  6.5 19.1 %copy-start.4 = (s32[1024,48]{0,1:T(8,128)S(1)}, s32[1024,48]{0,1:T(8,128)}, u32[]{:S(2)}) copy-start(s32[1024,48]{0,1:T(8,128)} %param.8) | copy-start | bytes 589828
  6.5 56.2 %all-gather.3.cloned.1.call-start = ((), (), s32[]{:S(2)}) async-start(), calls=%async_computation.8 | async-start | bytes 1769472 | tf_op jit(solution)/shard_map/all_gather | solution.py:206
  7.4 5.0 %collective-permute-start.8 = (bf16[32,768]{1,0:T(8,128)(2,1)S(1)}, bf16[32,768]{1,0:T(8,128)(2,1)S(1)}, u32[]{:S(2)}, u32[]{:S(2)}) collective-permute-start(bf16[32,768]{1,0:T(8,128)(2,1)S(1)} %get-tuple-element.132), channel_id=1, source_target_pairs={{1,0},{2,1},{3,2},{0,3},{5,4},{6,5},{7,6},{4,7},{9,8},{10,9},{11,1... | collective-permute-start | bytes 147464 | tf_op jit(solution)/shard_map/ppermute | solution.py:34
  9.7 5.6 %collective-permute-start.9 = (bf16[32,768]{1,0:T(8,128)(2,1)S(1)}, bf16[32,768]{1,0:T(8,128)(2,1)S(1)}, u32[]{:S(2)}, u32[]{:S(2)}) collective-permute-start(bf16[32,768]{1,0:T(8,128)(2,1)S(1)} %get-tuple-element.132), channel_id=1, source_target_pairs={{2,0},{3,1},{0,2},{1,3},{6,4},{7,5},{4,6},{5,7},{10,8},{11,9},{8,1... | collective-permute-start | bytes 147464 | tf_op jit(solution)/shard_map/ppermute | solution.py:34
  10.5 4.7 %collective-permute-start.10 = (bf16[32,768]{1,0:T(8,128)(2,1)S(1)}, bf16[32,768]{1,0:T(8,128)(2,1)S(1)}, u32[]{:S(2)}, u32[]{:S(2)}) collective-permute-start(bf16[32,768]{1,0:T(8,128)(2,1)S(1)} %get-tuple-element.132), channel_id=1, source_target_pairs={{3,0},{0,1},{1,2},{2,3},{7,4},{4,5},{5,6},{6,7},{11,8},{8,9},{9,10... | collective-permute-start | bytes 147464 | tf_op jit(solution)/shard_map/ppermute | solution.py:34
  16.8 22.5 %all-to-all-start.2 = ((bf16[8,32,768]{2,1,0:T(8,128)(2,1)}), bf16[8,32,768]{2,1,0:T(8,128)(2,1)S(1)}, u32[]{:S(2)}, u32[]{:S(2)}) async-start(bf16[8,32,768]{2,1,0:T(8,128)(2,1)} %broadcast_in_dim.58), calls=%async_computation.2 | async-start | bytes 786432 | tf_op jit(solution)/shard_map/all_to_all | solution.py:19
  25.9 36.8 %copy-start.6 = (f32[12,128]{1,0:T(8,128)S(1)}, f32[12,128]{1,0:T(8,128)}, u32[]{:S(2)}) copy-start(f32[12,128]{1,0:T(8,128)} %param.10) | copy-start | bytes 18436
  40.7 22.0 %all-to-all-start.3 = ((bf16[4,8,32,768]{3,2,1,0:T(8,128)(2,1)}), bf16[4,8,32,768]{3,2,1,0:T(8,128)(2,1)}, u32[]{:S(2)}, u32[]{:S(2)}) async-start(bf16[4,8,32,768]{3,2,1,0:T(8,128)(2,1)} %broadcast_in_dim.59), calls=%async_computation.3 | async-start | bytes 3145728 | tf_op jit(solution)/shard_map/all_to_all | solution.py:19
  49.5 112.5 %reduce-scatter.2.cloned.1.call-start = ((), (), s32[]{:S(2)}) async-start(), calls=%async_computation.7 | async-start | bytes 1769472 | tf_op jit(solution)/shard_map/reduce_scatter | solution.py:255
  85.1 1.8 collective-permute-start
  87.0 6.1 %collective-permute-start.1 = (bf16[384,128]{1,0:T(8,128)(2,1)S(1)}, bf16[384,128]{1,0:T(8,128)(2,1)S(1)}, u32[]{:S(2)}, u32[]{:S(2)}) collective-permute-start(bf16[384,128]{1,0:T(8,128)(2,1)S(1)} %get-tuple-element.125), channel_id=1, source_target_pairs={{192,0},{0,64},{64,128},{128,192},{193,1},{1,65},{65,129},{129,193... | collective-permute-start | bytes 294920 | tf_op jit(solution)/shard_map/cond/branch_1_fun/ppermute | solution.py:34
  88.8 7.6 %collective-permute-start.2 = (bf16[384,128]{1,0:T(8,128)(2,1)S(1)}, bf16[384,128]{1,0:T(8,128)(2,1)S(1)}, u32[]{:S(2)}, u32[]{:S(2)}) collective-permute-start(bf16[384,128]{1,0:T(8,128)(2,1)S(1)} %get-tuple-element.127), channel_id=1, source_target_pairs={{128,0},{192,64},{0,128},{64,192},{129,1},{193,65},{1,129},{65,193... | collective-permute-start | bytes 294920 | tf_op jit(solution)/shard_map/cond/branch_1_fun/ppermute | solution.py:34
  91.5 4.9 %collective-permute-start.3 = (bf16[384,128]{1,0:T(8,128)(2,1)S(1)}, bf16[384,128]{1,0:T(8,128)(2,1)S(1)}, u32[]{:S(2)}, u32[]{:S(2)}) collective-permute-start(bf16[384,128]{1,0:T(8,128)(2,1)S(1)} %get-tuple-element.126), channel_id=1, source_target_pairs={{64,0},{128,64},{192,128},{0,192},{65,1},{129,65},{193,129},{1,193... | collective-permute-start | bytes 294920 | tf_op jit(solution)/shard_map/cond/branch_1_fun/ppermute | solution.py:34
  96.4 5.3 %collective-permute-start.4 = (bf16[384,128]{1,0:T(8,128)(2,1)S(1)}, bf16[384,128]{1,0:T(8,128)(2,1)S(1)}, u32[]{:S(2)}, u32[]{:S(2)}) collective-permute-start(bf16[384,128]{1,0:T(8,128)(2,1)S(1)} %get-tuple-element.122), channel_id=1, source_target_pairs={{64,0},{128,64},{192,128},{0,192},{65,1},{129,65},{193,129},{1,193... | collective-permute-start | bytes 294920 | tf_op jit(solution)/shard_map/cond/branch_1_fun/ppermute | solution.py:34
  98.9 6.2 %collective-permute-start.5 = (bf16[384,128]{1,0:T(8,128)(2,1)S(1)}, bf16[384,128]{1,0:T(8,128)(2,1)S(1)}, u32[]{:S(2)}, u32[]{:S(2)}) collective-permute-start(bf16[384,128]{1,0:T(8,128)(2,1)S(1)} %get-tuple-element.122), channel_id=1, source_target_pairs={{128,0},{192,64},{0,128},{64,192},{129,1},{193,65},{1,129},{65,193... | collective-permute-start | bytes 294920 | tf_op jit(solution)/shard_map/cond/branch_1_fun/ppermute | solution.py:34
  99.8 6.2 %collective-permute-start.6 = (bf16[384,128]{1,0:T(8,128)(2,1)S(1)}, bf16[384,128]{1,0:T(8,128)(2,1)S(1)}, u32[]{:S(2)}, u32[]{:S(2)}) collective-permute-start(bf16[384,128]{1,0:T(8,128)(2,1)S(1)} %get-tuple-element.122), channel_id=1, source_target_pairs={{192,0},{0,64},{64,128},{128,192},{193,1},{1,65},{65,129},{129,193... | collective-permute-start | bytes 294920 | tf_op jit(solution)/shard_map/cond/branch_1_fun/ppermute | solution.py:34
  106.1 1.8 collective-permute-start.7
  112.8 1.6 copy-start.2
  114.4 2.3 %copy-start = (bf16[12,128,1536]{2,1,0:T(8,128)(2,1)S(1)}, bf16[12,128,1536]{2,1,0:T(8,128)(2,1)}, u32[]{:S(2)}) copy-start(bf16[12,128,1536]{2,1,0:T(8,128)(2,1)} %w_ref.3) | copy-start | bytes 14155780
  116.8 8.4 %copy-start.3 = (bf16[1024,1536]{1,0:T(8,128)(2,1)S(1)}, bf16[1024,1536]{1,0:T(8,128)(2,1)}, u32[]{:S(2)}) copy-start(bf16[1024,1536]{1,0:T(8,128)(2,1)} %copy-done.2) | copy-start | bytes 9437188
  125.2 2.3 %copy-start.1 = (bf16[12,128,1536]{2,1,0:T(8,128)(2,1)S(1)}, bf16[12,128,1536]{2,1,0:T(8,128)(2,1)}, u32[]{:S(2)}) copy-start(bf16[12,128,1536]{2,1,0:T(8,128)(2,1)} %w_ref.3) | copy-start | bytes 14155780
  158.0 18.2 %all-to-all-start.5 = ((bf16[8,32,768]{2,1,0:T(8,128)(2,1)}), bf16[8,32,768]{2,1,0:T(8,128)(2,1)S(1)}, u32[]{:S(2)}, u32[]{:S(2)}) async-start(bf16[8,32,768]{2,1,0:T(8,128)(2,1)} %reduce_sum.59), calls=%async_computation.5 | async-start | bytes 786432 | tf_op jit(solution)/shard_map/all_to_all | solution.py:25
  162.9 13.3 %collective-permute-start.11 = (bf16[32,768]{1,0:T(8,128)(2,1)S(1)}, bf16[32,768]{1,0:T(8,128)(2,1)S(1)}, u32[]{:S(2)}, u32[]{:S(2)}) collective-permute-start(bf16[32,768]{1,0:T(8,128)(2,1)S(1)} %get-tuple-element.128), channel_id=1, source_target_pairs={{3,0},{0,1},{1,2},{2,3},{7,4},{4,5},{5,6},{6,7},{11,8},{8,9},{9,10... | collective-permute-start | bytes 147464 | tf_op jit(solution)/shard_map/ppermute | solution.py:34
  163.7 12.5 %collective-permute-start.12 = (bf16[32,768]{1,0:T(8,128)(2,1)S(1)}, bf16[32,768]{1,0:T(8,128)(2,1)S(1)}, u32[]{:S(2)}, u32[]{:S(2)}) collective-permute-start(bf16[32,768]{1,0:T(8,128)(2,1)S(1)} %get-tuple-element.130), channel_id=1, source_target_pairs={{2,0},{3,1},{0,2},{1,3},{6,4},{7,5},{4,6},{5,7},{10,8},{11,9},{8,1... | collective-permute-start | bytes 147464 | tf_op jit(solution)/shard_map/ppermute | solution.py:34
  166.5 9.8 %collective-permute-start.13 = (bf16[32,768]{1,0:T(8,128)(2,1)S(1)}, bf16[32,768]{1,0:T(8,128)(2,1)S(1)}, u32[]{:S(2)}, u32[]{:S(2)}) collective-permute-start(bf16[32,768]{1,0:T(8,128)(2,1)S(1)} %get-tuple-element.129), channel_id=1, source_target_pairs={{1,0},{2,1},{3,2},{0,3},{5,4},{6,5},{7,6},{4,7},{9,8},{10,9},{11,1... | collective-permute-start | bytes 147464 | tf_op jit(solution)/shard_map/ppermute | solution.py:34
Sparse Core Ops, SparseCore 0:
  16.1 43.1 all-gather.2
  125.3 35.9 reduce-scatter.1
